TPU v7x, 256 devices: a whole 4x4x8 slice. The times are simulated.
256 devices in a mesh: lev: 32 (over y, x, core), lon: 8 (over z).
Axes of the slice: x: 4, y: 4, z: 8, core: 2. Of those that a mesh axis runs over, the one named last changes fastest.
Arguments:
- levels_in: bfloat16 [128, 192, 96, 128], P('lev', None, 'lon'), may hold values from -6 to 6
- slab_levels: int32 [32], replicated, may hold values from 1 to 4, 64 in all
- shifts: int32 [32], replicated, may hold values from 0 to 11
- gain_col: float32 [128], replicated, may hold values from 0.1 to 1.9
- w_col_qkv: bfloat16 [128, 384], replicated
- w_col_out: bfloat16 [128, 128], replicated, may hold values from -0.5 to 0.5
- gain_win: float32 [128], replicated, may hold values from 0.1 to 1.9
- w_win_qkv: bfloat16 [128, 384], replicated
- w_win_out: bfloat16 [128, 128], replicated, may hold values from -0.5 to 0.5
- gain_mlp: float32 [128], replicated, may hold values from 0.1 to 1.9
- w_up: bfloat16 [128, 512], replicated, may hold values from -0.5 to 0.5
- w_down: bfloat16 [512, 128], replicated, may hold values from -0.25 to 0.25
Outputs:
- levels_out: bfloat16 [128, 192, 96, 128], P('lev', None, 'lon')
All inputs are finite; a program needn't handle non-finite values.
Results may differ from a plain program's by a relative error of at most 0.0095.
Values may be sent and summed in bfloat16 or wider, within the bound.
A program may use at most 128 MiB of HBM per device.

v0:
```python
import functools
import math

import jax
import jax.numpy as jnp
from jax import lax
from jax.experimental import pallas as pl
from jax.experimental.pallas import tpu as pltpu
from jax.sharding import PartitionSpec as P

HEADS = 4
EPS = 1e-05
MESH = pl.DeviceIdType.MESH
F32 = jnp.float32
BF16 = jnp.bfloat16

SLOTS = 4
LON = 12
LAT = 6
HALF = LON // 2
LEVD = 32
LEV = 64
LATS = LAT * LEVD
C = 128
COLS = HALF * LAT
ROWS_IN = SLOTS * LON
ROWS_OUT = SLOTS * COLS
HROWS = LEV * COLS
PAIR = 4 * COLS
PAIRS = LEV // 4
GROUPS = 4
GROUP = PAIRS // GROUPS
HCOL = HALF * LEV
SCALE = math.log2(math.e) / math.sqrt(C // HEADS)


def norm(v, gain):
    centred = v - jnp.mean(v, -1, keepdims=True)
    spread = jnp.mean(centred * centred, -1, keepdims=True)
    return (centred * lax.rsqrt(spread + EPS) * gain).astype(BF16)


def dot(a, b):
    return jnp.dot(a, b, preferred_element_type=F32)


def dot_nt(a, b):
    return lax.dot_general(a, b, (((1,), (1,)), ((), ())), preferred_element_type=F32)


def head_masks(rows):
    lane = lax.broadcasted_iota(jnp.int32, (rows, C), 1)
    return [(lane // (C // HEADS)) == h for h in range(HEADS)]


def attend(q, k, v, masks):
    n = q.shape[0]
    value = jnp.concatenate([v, jnp.ones((n, C), BF16)], 1)
    total = None
    for h in range(HEADS):
        scores = dot_nt(jnp.where(masks[h], q, jnp.zeros_like(q)), k)
        top = jnp.max(scores, -1, keepdims=True)
        probs = jnp.exp2((scores - top) * SCALE).astype(BF16)
        both = dot(probs, value)
        part = both[:, :C] / both[:, C:]
        total = part if total is None else jnp.where(masks[h], part, total)
    return total


def plane_target(me, step):
    core, x, y = lax.rem(me, 2), lax.rem(me // 2, 4), me // 8
    dc, dx, dy = lax.rem(step, 2), lax.rem(step // 2, 4), step // 8
    return (lax.rem(y + dy, 4) * 4 + lax.rem(x + dx, 4)) * 2 + lax.rem(core + dc, 2)


def kernel(
    counts_ref, shifts_ref, x_ref, gcol_ref, wcq_ref, wco_ref, gwin_ref, wwq_ref, wwo_ref,
    gmlp_ref, wup_ref, wdn_ref, out_ref,
    rowoff, starts, big, sendbuf, recv, r32, xl, srow, after, hsend, hrecv, wtok, attd, back,
    blk, msg, got,
    in_send, in_recv, h_send, h_recv, b_send, b_recv, o_send, o_recv,
):
    me = lax.axis_index("lev")
    z = lax.axis_index("lon")
    east = lax.rem(z + 1, 8)
    west = lax.rem(z + 7, 8)

    barrier = pltpu.get_barrier_semaphore()

    def greet(step, _):
        pl.semaphore_signal(barrier, inc=1, device_id={"lev": plane_target(me, step)}, device_id_type=MESH)
        return 0

    lax.fori_loop(1, LEVD, greet, 0)
    for side in (east, west):
        pl.semaphore_signal(barrier, inc=1, device_id={"lon": side}, device_id_type=MESH)

    def widen(n, _):
        big[pl.ds(pl.multiple_of(n * LATS, LATS), LATS), :] = x_ref[n].astype(F32)
        return 0

    lax.fori_loop(0, ROWS_IN, widen, 0)
    pl.semaphore_wait(barrier, LEVD - 1 + 2)

    def in_copy(i, dest):
        return pltpu.make_async_remote_copy(
            src_ref=sendbuf.at[i, dest], dst_ref=recv.at[i, me],
            send_sem=in_send.at[i], recv_sem=in_recv.at[i],
            device_id={"lev": dest}, device_id_type=MESH,
        )

    def send_chunk(i, _):
        def one(step, _):
            dest = plane_target(me, LEVD - step)
            sendbuf[i, dest] = big[pl.ds(dest * LAT + i, ROWS_IN, stride=LATS), :].astype(BF16)
            in_copy(i, dest).start()
            return 0

        lax.fori_loop(1, LEVD, one, 0)
        recv[i, me] = big[pl.ds(me * LAT + i, ROWS_IN, stride=LATS), :].astype(BF16)
        return 0

    lax.fori_loop(0, LAT, send_chunk, 0)

    def place(level, carry):
        slab, slot = carry
        rowoff[level] = jnp.minimum(slab, LEVD - 1) * ROWS_IN + jnp.minimum(slot, SLOTS - 1) * LON
        more = slot + 1
        ends = more >= counts_ref[jnp.minimum(slab, LEVD - 1)]
        return jnp.where(ends, slab + 1, slab), jnp.where(ends, 0, more)

    lax.fori_loop(0, LEV, place, (jnp.int32(0), jnp.int32(0)))

    def begin(slab, start):
        starts[slab] = jnp.minimum(start, LEV - 1)
        return start + counts_ref[slab]

    lax.fori_loop(0, LEVD, begin, jnp.int32(0))

    def shift_rows(level, _):
        srow[pl.ds(level, 1), :] = jnp.full((1, C), shifts_ref[level // 2], jnp.int32)
        return 0

    lax.fori_loop(0, LEV, shift_rows, 0)

    def halo_copy(i, half, side):
        return pltpu.make_async_remote_copy(
            src_ref=hsend.at[i, half], dst_ref=hrecv.at[i, half],
            send_sem=h_send.at[i, half], recv_sem=h_recv.at[i, half],
            device_id={"lon": side}, device_id_type=MESH,
        )

    masks64 = head_masks(LEV)

    def column_chunk(i, _):
        pltpu.make_async_copy(
            recv.at[i, pl.ds(0, LEVD - 1)], recv.at[i, pl.ds(0, LEVD - 1)], in_recv.at[i]
        ).wait()

        def widen_in(d, _):
            r32[pl.ds(pl.multiple_of(d * ROWS_IN, ROWS_IN), ROWS_IN), :] = recv[i, d].astype(F32)
            return 0

        lax.fori_loop(0, LEVD, widen_in, 0)

        def pick(level, _):
            xl[pl.ds(pl.multiple_of(level * 16, 16), 16), :] = r32[pl.ds(rowoff[level], 16), :]
            return 0

        lax.fori_loop(0, LEV, pick, 0, unroll=8)

        for half in range(2):
            for first in range(0, HALF, 3):
                lons = [half * HALF + first + n for n in range(3)]
                cols = jnp.concatenate([xl[pl.ds(lon, LEV, stride=16), :] for lon in lons], 0)
                packed = dot(norm(cols, gcol_ref[...]), wcq_ref[...]).astype(BF16)
                parts = []
                for n in range(3):
                    one = packed[n * LEV:(n + 1) * LEV]
                    parts.append(attend(one[:, :C], one[:, C:2 * C], one[:, 2 * C:], masks64))
                attended = jnp.concatenate(parts, 0).astype(BF16)
                done = cols + dot(attended, wco_ref[...])
                normed = norm(done, gwin_ref[...])
                for n in range(3):
                    at = half * HROWS + i * HALF + first + n
                    after[pl.ds(at, LEV, stride=COLS), :] = done[n * LEV:(n + 1) * LEV]
                    hsend[i, half, pl.ds((first + n) * LEV, LEV), :] = normed[n * LEV:(n + 1) * LEV]
            halo_copy(i, half, west if half == 0 else east).start()
        return 0

    def merge_chunk(i, _):
        for half in range(2):
            halo_copy(i, half, west if half == 0 else east).wait_recv()
            for n in range(HALF):
                lon = half * HALF + n
                shift = srow[...]
                own = (lon >= shift) == (shift <= HALF)
                mine = hsend[i, half, pl.ds(n * LEV, LEV), :].astype(F32)
                other = hrecv[i, half, pl.ds(n * LEV, LEV), :].astype(F32)
                at = half * HROWS + i * HALF + n
                wtok[pl.ds(at, LEV, stride=COLS), :] = jnp.where(own, mine, other)
        return 0

    def both_chunks(i, _):
        column_chunk(i, 0)
        merge_chunk(i - 1, 0)
        return 0

    column_chunk(0, 0)
    lax.fori_loop(1, LAT, both_chunks, 0)
    merge_chunk(LAT - 1, 0)

    masks144 = head_masks(PAIR)

    def back_copy(g, half, side):
        part = pl.ds(pl.multiple_of(g * (GROUP * PAIR), GROUP * PAIR), GROUP * PAIR)
        return pltpu.make_async_remote_copy(
            src_ref=attd.at[half, part], dst_ref=back.at[half, part],
            send_sem=b_send.at[half, g], recv_sem=b_recv.at[half, g],
            device_id={"lon": side}, device_id_type=MESH,
        )

    def window_pair(p, _):
        at = pl.multiple_of(p * PAIR, PAIR)
        quarters = []
        for band in range(2):
            for half in range(2):
                quarters.append(wtok[pl.ds(at + half * HROWS + band * (PAIR // 2), PAIR // 2), :])
        tokens = jnp.concatenate(quarters, 0).astype(BF16)
        packed = dot(tokens, wwq_ref[...]).astype(BF16)
        bands = []
        for band in range(2):
            one = packed[band * PAIR:(band + 1) * PAIR]
            bands.append(attend(one[:, :C], one[:, C:2 * C], one[:, 2 * C:], masks144))
        for half in range(2):
            rows = slice(half * (PAIR // 2), (half + 1) * (PAIR // 2))
            attd[half, pl.ds(at, PAIR), :] = jnp.concatenate([b[rows] for b in bands], 0).astype(BF16)
        return 0

    def window_group(g, _):
        lax.fori_loop(g * GROUP, (g + 1) * GROUP, window_pair, 0)
        back_copy(g, 0, east).start()
        back_copy(g, 1, west).start()
        return 0

    lax.fori_loop(0, GROUPS, window_group, 0)

    def out_copy(half, dest):
        return pltpu.make_async_remote_copy(
            src_ref=msg.at[half, dest], dst_ref=got.at[half, me],
            send_sem=o_send.at[half], recv_sem=o_recv.at[half],
            device_id={"lev": dest}, device_id_type=MESH,
        )

    row = lax.broadcasted_iota(jnp.int32, (PAIR, C), 0)
    for half in range(2):
        lon_of_row = lax.rem(row, HALF) + half * HALF

        def feed_pair(p, _):
            at = pl.multiple_of(p * PAIR, PAIR)
            shift = jnp.where(row < PAIR // 2, shifts_ref[2 * p], shifts_ref[2 * p + 1])
            own = (lon_of_row >= shift) == (shift <= HALF)
            attended = jnp.where(
                own, attd[half, pl.ds(at, PAIR), :].astype(F32), back[half, pl.ds(at, PAIR), :].astype(F32)
            ).astype(BF16)
            stay = after[pl.ds(at + half * HROWS, PAIR), :] + dot(attended, wwo_ref[...])
            hidden = jax.nn.gelu(dot(norm(stay, gmlp_ref[...]), wup_ref[...]), approximate=True)
            blk[half, pl.ds(at, PAIR), :] = stay + dot(hidden.astype(BF16), wdn_ref[...])
            return 0

        def feed_group(g, _):
            back_copy(g, half, east if half == 0 else west).wait_recv()
            lax.fori_loop(g * GROUP, (g + 1) * GROUP, feed_pair, 0)
            return 0

        blk[half, pl.ds(HROWS, PAIR), :] = jnp.zeros((PAIR, C), F32)
        lax.fori_loop(0, GROUPS, feed_group, 0)

        def block_for(dest):
            rows = blk[half, pl.ds(starts[dest] * COLS, ROWS_OUT), :]
            return jnp.where(row < counts_ref[dest] * COLS, rows, 0.0).astype(BF16)

        def send_out(step, _):
            dest = plane_target(me, LEVD - step)
            msg[half, dest] = block_for(dest)
            out_copy(half, dest).start()
            return 0

        lax.fori_loop(1, LEVD, send_out, 0)
        got[half, me] = block_for(me)

    for half in range(2):
        pltpu.make_async_copy(
            got.at[half, pl.ds(0, LEVD - 1)], got.at[half, pl.ds(0, LEVD - 1)], o_recv.at[half]
        ).wait()

        def widen_out(e, _):
            big[pl.ds(pl.multiple_of(e * ROWS_OUT, ROWS_OUT), ROWS_OUT), :] = got[half, e].astype(F32)
            return 0

        lax.fori_loop(0, LEVD, widen_out, 0)

        def unpack(n, _):
            slot, lon = n // HALF, lax.rem(n, HALF)
            for i in range(LAT):
                r32[pl.ds(i, LEVD, stride=LAT), :] = big[
                    pl.ds(slot * COLS + i * HALF + lon, LEVD, stride=ROWS_OUT), :
                ]
            out_ref[slot * LON + half * HALF + lon] = r32[pl.ds(0, LATS), :].astype(BF16)
            return 0

        lax.fori_loop(0, SLOTS * HALF, unpack, 0)

    for i in range(LAT):
        pltpu.make_async_copy(
            sendbuf.at[i, pl.ds(0, LEVD - 1)], sendbuf.at[i, pl.ds(0, LEVD - 1)], in_send.at[i]
        ).wait()
        halo_copy(i, 0, west).wait_send()
        halo_copy(i, 1, east).wait_send()
    for g in range(GROUPS):
        back_copy(g, 0, east).wait_send()
        back_copy(g, 1, west).wait_send()
    for half in range(2):
        pltpu.make_async_copy(
            msg.at[half, pl.ds(0, LEVD - 1)], msg.at[half, pl.ds(0, LEVD - 1)], o_send.at[half]
        ).wait()


def per_device(
    levels_in, slab_levels, shifts, gain_col, w_col_qkv, w_col_out, gain_win, w_win_qkv, w_win_out,
    gain_mlp, w_up, w_down,
):
    x = levels_in.transpose(0, 2, 1, 3).reshape(ROWS_IN, LATS, C)
    smem = pl.BlockSpec(memory_space=pltpu.SMEM)
    vmem = pl.BlockSpec(memory_space=pltpu.VMEM)
    dma = pltpu.SemaphoreType.DMA
    out = pl.pallas_call(
        kernel,
        out_shape=jax.ShapeDtypeStruct((ROWS_IN, LATS, C), BF16),
        in_specs=[smem, smem] + [vmem] * 10,
        out_specs=vmem,
        scratch_shapes=[
            pltpu.SMEM((LEV,), jnp.int32),
            pltpu.SMEM((LEVD,), jnp.int32),
            pltpu.VMEM((ROWS_IN * LATS, C), F32),
            pltpu.VMEM((LAT, LEVD, ROWS_IN, C), BF16),
            pltpu.VMEM((LAT, LEVD, ROWS_IN, C), BF16),
            pltpu.VMEM((LEVD * ROWS_IN + 8, C), F32),
            pltpu.VMEM((LEV * 16, C), F32),
            pltpu.VMEM((LEV, C), jnp.int32),
            pltpu.VMEM((2 * HROWS, C), F32),
            pltpu.VMEM((LAT, 2, HCOL, C), BF16),
            pltpu.VMEM((LAT, 2, HCOL, C), BF16),
            pltpu.VMEM((2 * HROWS, C), F32),
            pltpu.VMEM((2, HROWS, C), BF16),
            pltpu.VMEM((2, HROWS, C), BF16),
            pltpu.VMEM((2, HROWS + PAIR, C), F32),
            pltpu.VMEM((2, LEVD, ROWS_OUT, C), BF16),
            pltpu.VMEM((2, LEVD, ROWS_OUT, C), BF16),
            dma((LAT,)), dma((LAT,)),
            dma((LAT, 2)), dma((LAT, 2)),
            dma((2, GROUPS)), dma((2, GROUPS)),
            dma((2,)), dma((2,)),
        ],
        compiler_params=pltpu.CompilerParams(
            collective_id=0, has_side_effects=True, vmem_limit_bytes=56 * 1024 * 1024
        ),
    )(
        slab_levels, shifts, x, gain_col.reshape(1, C), w_col_qkv, w_col_out, gain_win.reshape(1, C),
        w_win_qkv, w_win_out, gain_mlp.reshape(1, C), w_up, w_down,
    )
    return out.reshape(SLOTS, LON, LATS, C).transpose(0, 2, 1, 3)


def solution(mesh):
    placed = (P("lev", None, "lon", None),) + (P(),) * 11
    return jax.shard_map(
        per_device,
        mesh=mesh,
        in_specs=placed,
        out_specs=P("lev", None, "lon", None),
        check_vma=False,
    )
```

profile of v0, /device:TPU:1, one launch (start us, length us, event | category | flops | bytes accessed | tf_op | source)
XLA Modules:
  0.0 112.3 jit_solution(11683952011695094937)
XLA Ops:
  0.0 109.1 %shard_map.118 = bf16[48,192,128]{2,1,0:T(8,128)(2,1)} custom-call(s32[32]{0:T(128)} %counts_ref.1, s32[32]{0:T(128)} %shifts_ref.1, bf16[48,192,128]{2,1,0:T(8,128)(2,1)} %bitcast.10, f32[1,128]{1,0:T(1,128)} %bitcast.11, bf16[128,384]{1,0:T(8,128)(2,1)} %wcq_ref.1, bf16[128,128]{1,0:T(8,128)(2,1)} %wco_ref.1, f32[1,128]{1,0:T(1,128)} %bitcast.12, ...), custom_call_target="tpu_custom_call" | custom-call | tf_op jit(solution)/shard_map/pallas_call | solution.py:337
  109.1 3.2 %copy.14 = bf16[4,192,12,128]{3,1,2,0:T(8,128)(2,1)} copy(bf16[4,192,12,128]{3,1,2,0:T(8,128)(2,1)} %bitcast.9) | data formatting | bytes 4718592
where the time goes:
time: 112 us
  Pallas kernels  109 us (97%)
  local copies, waits for them, and re-layouts  3.22 us (3%)
    pallas_call x1, Pallas kernels, per_device(): pl.pallas_call(kernel, out_shape=jax.ShapeDtypeStruct((ROWS_IN, LATS, C),...  109 us
    unnamed x1, local copies, waits for them, and re-layouts  3.22 us

commit v1 on v0

--- a/solution.py
+++ b/solution.py
@@ -31,6 +31,11 @@
 GROUPS = 4
 GROUP = PAIRS // GROUPS
 HCOL = HALF * LEV
+FEED = 4
+WIN = 4
+COLG = 6
+GELU_A = math.sqrt(2.0 / math.pi)
+GELU_B = GELU_A * 0.044715
 SCALE = math.log2(math.e) / math.sqrt(C // HEADS)
 
 
@@ -56,15 +61,21 @@
 def attend(q, k, v, masks):
     n = q.shape[0]
     value = jnp.concatenate([v, jnp.ones((n, C), BF16)], 1)
-    total = None
+    over, under = None, None
     for h in range(HEADS):
         scores = dot_nt(jnp.where(masks[h], q, jnp.zeros_like(q)), k)
         top = jnp.max(scores, -1, keepdims=True)
         probs = jnp.exp2((scores - top) * SCALE).astype(BF16)
         both = dot(probs, value)
-        part = both[:, :C] / both[:, C:]
-        total = part if total is None else jnp.where(masks[h], part, total)
-    return total
+        over = both[:, :C] if h == 0 else jnp.where(masks[h], both[:, :C], over)
+        under = both[:, C:] if h == 0 else jnp.where(masks[h], both[:, C:], under)
+    return over / under
+
+
+def gelu(v):
+    inner = v * (GELU_A + GELU_B * (v * v))
+    half = 0.5 * v
+    return half * jnp.tanh(inner) + half
 
 
 def plane_target(me, step):
@@ -77,7 +88,7 @@
     counts_ref, shifts_ref, x_ref, gcol_ref, wcq_ref, wco_ref, gwin_ref, wwq_ref, wwo_ref,
     gmlp_ref, wup_ref, wdn_ref, out_ref,
     rowoff, starts, big, sendbuf, recv, r32, xl, srow, after, hsend, hrecv, wtok, attd, back,
-    blk, msg, got,
+    mask, blk, msg, got,
     in_send, in_recv, h_send, h_recv, b_send, b_recv, o_send, o_recv,
 ):
     me = lax.axis_index("lev")
@@ -143,6 +154,17 @@
 
     lax.fori_loop(0, LEV, shift_rows, 0)
 
+    row = lax.broadcasted_iota(jnp.int32, (PAIR, C), 0)
+
+    def own_rows(p, _):
+        shift = jnp.where(row < PAIR // 2, shifts_ref[2 * p], shifts_ref[2 * p + 1])
+        for half in range(2):
+            own = (lax.rem(row, HALF) + half * HALF >= shift) == (shift <= HALF)
+            mask[half, pl.ds(pl.multiple_of(p * PAIR, PAIR), PAIR), :] = own.astype(jnp.int32)
+        return 0
+
+    lax.fori_loop(0, PAIRS, own_rows, 0)
+
     def halo_copy(i, half, side):
         return pltpu.make_async_remote_copy(
             src_ref=hsend.at[i, half], dst_ref=hrecv.at[i, half],
@@ -170,18 +192,18 @@
         lax.fori_loop(0, LEV, pick, 0, unroll=8)
 
         for half in range(2):
-            for first in range(0, HALF, 3):
-                lons = [half * HALF + first + n for n in range(3)]
+            for first in range(0, HALF, COLG):
+                lons = [half * HALF + first + n for n in range(COLG)]
                 cols = jnp.concatenate([xl[pl.ds(lon, LEV, stride=16), :] for lon in lons], 0)
                 packed = dot(norm(cols, gcol_ref[...]), wcq_ref[...]).astype(BF16)
                 parts = []
-                for n in range(3):
+                for n in range(COLG):
                     one = packed[n * LEV:(n + 1) * LEV]
                     parts.append(attend(one[:, :C], one[:, C:2 * C], one[:, 2 * C:], masks64))
                 attended = jnp.concatenate(parts, 0).astype(BF16)
                 done = cols + dot(attended, wco_ref[...])
                 normed = norm(done, gwin_ref[...])
-                for n in range(3):
+                for n in range(COLG):
                     at = half * HROWS + i * HALF + first + n
                     after[pl.ds(at, LEV, stride=COLS), :] = done[n * LEV:(n + 1) * LEV]
                     hsend[i, half, pl.ds((first + n) * LEV, LEV), :] = normed[n * LEV:(n + 1) * LEV]
@@ -221,24 +243,25 @@
         )
 
     def window_pair(p, _):
-        at = pl.multiple_of(p * PAIR, PAIR)
+        rows = WIN * PAIR
+        at = pl.multiple_of(p * rows, rows)
         quarters = []
-        for band in range(2):
+        for band in range(2 * WIN):
             for half in range(2):
                 quarters.append(wtok[pl.ds(at + half * HROWS + band * (PAIR // 2), PAIR // 2), :])
         tokens = jnp.concatenate(quarters, 0).astype(BF16)
         packed = dot(tokens, wwq_ref[...]).astype(BF16)
         bands = []
-        for band in range(2):
+        for band in range(2 * WIN):
             one = packed[band * PAIR:(band + 1) * PAIR]
             bands.append(attend(one[:, :C], one[:, C:2 * C], one[:, 2 * C:], masks144))
         for half in range(2):
-            rows = slice(half * (PAIR // 2), (half + 1) * (PAIR // 2))
-            attd[half, pl.ds(at, PAIR), :] = jnp.concatenate([b[rows] for b in bands], 0).astype(BF16)
+            part = slice(half * (PAIR // 2), (half + 1) * (PAIR // 2))
+            attd[half, pl.ds(at, rows), :] = jnp.concatenate([b[part] for b in bands], 0).astype(BF16)
         return 0
 
     def window_group(g, _):
-        lax.fori_loop(g * GROUP, (g + 1) * GROUP, window_pair, 0)
+        lax.fori_loop(g * (GROUP // WIN), (g + 1) * (GROUP // WIN), window_pair, 0)
         back_copy(g, 0, east).start()
         back_copy(g, 1, west).start()
         return 0
@@ -252,25 +275,24 @@
             device_id={"lev": dest}, device_id_type=MESH,
         )
 
-    row = lax.broadcasted_iota(jnp.int32, (PAIR, C), 0)
     for half in range(2):
-        lon_of_row = lax.rem(row, HALF) + half * HALF
 
         def feed_pair(p, _):
-            at = pl.multiple_of(p * PAIR, PAIR)
-            shift = jnp.where(row < PAIR // 2, shifts_ref[2 * p], shifts_ref[2 * p + 1])
-            own = (lon_of_row >= shift) == (shift <= HALF)
+            rows = FEED * PAIR
+            at = pl.multiple_of(p * rows, rows)
             attended = jnp.where(
-                own, attd[half, pl.ds(at, PAIR), :].astype(F32), back[half, pl.ds(at, PAIR), :].astype(F32)
+                mask[half, pl.ds(at, rows), :] > 0,
+                attd[half, pl.ds(at, rows), :].astype(F32),
+                back[half, pl.ds(at, rows), :].astype(F32),
             ).astype(BF16)
-            stay = after[pl.ds(at + half * HROWS, PAIR), :] + dot(attended, wwo_ref[...])
-            hidden = jax.nn.gelu(dot(norm(stay, gmlp_ref[...]), wup_ref[...]), approximate=True)
-            blk[half, pl.ds(at, PAIR), :] = stay + dot(hidden.astype(BF16), wdn_ref[...])
+            stay = after[pl.ds(at + half * HROWS, rows), :] + dot(attended, wwo_ref[...])
+            hidden = gelu(dot(norm(stay, gmlp_ref[...]), wup_ref[...]))
+            blk[half, pl.ds(at, rows), :] = stay + dot(hidden.astype(BF16), wdn_ref[...])
             return 0
 
         def feed_group(g, _):
             back_copy(g, half, east if half == 0 else west).wait_recv()
-            lax.fori_loop(g * GROUP, (g + 1) * GROUP, feed_pair, 0)
+            lax.fori_loop(g * (GROUP // FEED), (g + 1) * (GROUP // FEED), feed_pair, 0)
             return 0
 
         blk[half, pl.ds(HROWS, PAIR), :] = jnp.zeros((PAIR, C), F32)
@@ -354,6 +376,7 @@
             pltpu.VMEM((2 * HROWS, C), F32),
             pltpu.VMEM((2, HROWS, C), BF16),
             pltpu.VMEM((2, HROWS, C), BF16),
+            pltpu.VMEM((2, HROWS, C), jnp.int32),
             pltpu.VMEM((2, HROWS + PAIR, C), F32),
             pltpu.VMEM((2, LEVD, ROWS_OUT, C), BF16),
             pltpu.VMEM((2, LEVD, ROWS_OUT, C), BF16),

time: 112 us -> 100 us (0.89)
  Pallas kernels: 109 us -> 96.6 us
    pallas_call x1, Pallas kernels: 109 us -> 96.6 us  [per_device(): pl.pallas_call(kernel, out_shape=jax.ShapeDtypeStruct((ROWS_IN, LATS, C),...]
where the time goes in v1:
time: 100 us; the launch traced here: 99.8 us
  Pallas kernels  96.6 us (97%)
  local copies, waits for them, and re-layouts  3.22 us (3%)
    pallas_call x1, Pallas kernels, per_device(): pl.pallas_call(kernel, out_shape=jax.ShapeDtypeStruct((ROWS_IN, LATS, C),...  96.6 us
    unnamed x1, local copies, waits for them, and re-layouts  3.22 us

profile of v1, /device:TPU:1, one launch (start us, length us, event | category | flops | bytes accessed | tf_op | source)
XLA Modules:
  0.0 99.8 jit_solution(4625028941688873928)
XLA Ops:
  0.0 96.6 %shard_map.118 = bf16[48,192,128]{2,1,0:T(8,128)(2,1)} custom-call(s32[32]{0:T(128)} %counts_ref.1, s32[32]{0:T(128)} %shifts_ref.1, bf16[48,192,128]{2,1,0:T(8,128)(2,1)} %bitcast.10, f32[1,128]{1,0:T(1,128)} %bitcast.11, bf16[128,384]{1,0:T(8,128)(2,1)} %wcq_ref.1, bf16[128,128]{1,0:T(8,128)(2,1)} %wco_ref.1, f32[1,128]{1,0:T(1,128)} %bitcast.12, ...), custom_call_target="tpu_custom_call" | custom-call | tf_op jit(solution)/shard_map/pallas_call | solution.py:359
  96.6 3.2 %copy.14 = bf16[4,192,12,128]{3,1,2,0:T(8,128)(2,1)} copy(bf16[4,192,12,128]{3,1,2,0:T(8,128)(2,1)} %bitcast.9) | data formatting | bytes 4718592

commit v2 on v1

--- a/solution.py
+++ b/solution.py
@@ -33,7 +33,6 @@
 HCOL = HALF * LEV
 FEED = 4
 WIN = 4
-COLG = 6
 GELU_A = math.sqrt(2.0 / math.pi)
 GELU_B = GELU_A * 0.044715
 SCALE = math.log2(math.e) / math.sqrt(C // HEADS)
@@ -72,6 +71,47 @@
     return over / under
 
 
+def attend_short(q, k, v, masks, ones):
+    zero = jnp.zeros_like(k)
+    keys = jnp.concatenate([jnp.where(m, k, zero) for m in masks], 0)
+    values = jnp.concatenate([jnp.where(m, v, zero) for m in masks], 0)
+    scores = dot_nt(q, keys)
+    low = lax.broadcasted_iota(jnp.int32, (LEV, C), 1) < LEV
+    probs = []
+    for t in range(2):
+        part = scores[:, t * C:(t + 1) * C]
+        top = jnp.where(
+            low,
+            jnp.max(jnp.where(low, part, -jnp.inf), -1, keepdims=True),
+            jnp.max(jnp.where(low, -jnp.inf, part), -1, keepdims=True),
+        )
+        probs.append(jnp.exp2((part - top) * SCALE).astype(BF16))
+    both = dot(jnp.concatenate(probs, 1), jnp.concatenate([values, ones], 1))
+    return both[:, :C] / both[:, C:]
+
+
+def attend_long(q, k, v, masks, tail_masks, ones, tail_ones):
+    n = q.shape[0]
+    extra = n - C
+    km, kt, vm, vt = k[:C], k[C:], v[:C], v[C:]
+    zero, none = jnp.zeros_like(km), jnp.zeros_like(kt)
+    tail = dot_nt(q, jnp.concatenate([jnp.where(m[:extra], kt, none) for m in masks], 0))
+    tails = jnp.zeros((n, HEADS * extra), F32)
+    total = None
+    for h in range(HEADS):
+        scores = dot_nt(q, jnp.where(masks[h], km, zero))
+        mine = jnp.where(tail_masks[h], tail, -jnp.inf)
+        top = jnp.max(jnp.maximum(scores, jnp.concatenate([mine, jnp.full((n, C - HEADS * extra), -jnp.inf, F32)], 1)), -1, keepdims=True)
+        probs = jnp.exp2((scores - top) * SCALE).astype(BF16)
+        tails = jnp.where(tail_masks[h], top, tails)
+        part = dot(probs, jnp.concatenate([jnp.where(masks[h], vm, zero), ones[h]], 1))
+        total = part if total is None else total + part
+    probs = jnp.exp2((tail - tails) * SCALE).astype(BF16)
+    values = jnp.concatenate([jnp.where(m[:extra], vt, none) for m in masks], 0)
+    total = total + dot(probs, jnp.concatenate([values, tail_ones], 1))
+    return total[:, :C] / total[:, C:]
+
+
 def gelu(v):
     inner = v * (GELU_A + GELU_B * (v * v))
     half = 0.5 * v
@@ -85,11 +125,12 @@
 
 
 def kernel(
-    counts_ref, shifts_ref, x_ref, gcol_ref, wcq_ref, wco_ref, gwin_ref, wwq_ref, wwo_ref,
-    gmlp_ref, wup_ref, wdn_ref, out_ref,
-    rowoff, starts, big, sendbuf, recv, r32, xl, srow, after, hsend, hrecv, wtok, attd, back,
+    counts_ref, shifts_ref, x_ref, gcol_hbm, wcq_hbm, wco_hbm, gwin_hbm, wwq_hbm, wwo_hbm,
+    gmlp_hbm, wup_hbm, wdn_hbm, out_ref,
+    gcol_ref, wcq_ref, wco_ref, gwin_ref, wwq_ref, wwo_ref, gmlp_ref, wup_ref, wdn_ref,
+    rowoff, starts, xin, big, sendbuf, recv, r32, xl, srow, after, hsend, hrecv, wtok, attd, back,
     mask, blk, msg, got,
-    in_send, in_recv, h_send, h_recv, b_send, b_recv, o_send, o_recv,
+    x_sem, w_sem, in_send, in_recv, h_send, h_recv, b_send, b_recv, o_send, o_recv,
 ):
     me = lax.axis_index("lev")
     z = lax.axis_index("lon")
@@ -98,6 +139,21 @@
 
     barrier = pltpu.get_barrier_semaphore()
 
+    def x_copy(slot):
+        part = pl.ds(slot * LON, LON)
+        return pltpu.make_async_copy(x_ref.at[part], xin.at[part], x_sem.at[slot])
+
+    for slot in range(SLOTS):
+        x_copy(slot).start()
+    weights = [
+        pltpu.make_async_copy(far, near, w_sem.at[n])
+        for n, (far, near) in enumerate([
+            (gcol_hbm, gcol_ref), (wcq_hbm, wcq_ref), (wco_hbm, wco_ref), (gwin_hbm, gwin_ref),
+            (wwq_hbm, wwq_ref), (wwo_hbm, wwo_ref), (gmlp_hbm, gmlp_ref), (wup_hbm, wup_ref),
+            (wdn_hbm, wdn_ref),
+        ])
+    ]
+
     def greet(step, _):
         pl.semaphore_signal(barrier, inc=1, device_id={"lev": plane_target(me, step)}, device_id_type=MESH)
         return 0
@@ -107,10 +163,12 @@
         pl.semaphore_signal(barrier, inc=1, device_id={"lon": side}, device_id_type=MESH)
 
     def widen(n, _):
-        big[pl.ds(pl.multiple_of(n * LATS, LATS), LATS), :] = x_ref[n].astype(F32)
-        return 0
-
-    lax.fori_loop(0, ROWS_IN, widen, 0)
+        big[pl.ds(pl.multiple_of(n * LATS, LATS), LATS), :] = xin[n].astype(F32)
+        return 0
+
+    for slot in range(SLOTS):
+        x_copy(slot).wait()
+        lax.fori_loop(slot * LON, (slot + 1) * LON, widen, 0)
     pl.semaphore_wait(barrier, LEVD - 1 + 2)
 
     def in_copy(i, dest):
@@ -133,6 +191,9 @@
 
     lax.fori_loop(0, LAT, send_chunk, 0)
 
+    for weight in weights:
+        weight.start()
+
     def place(level, carry):
         slab, slot = carry
         rowoff[level] = jnp.minimum(slab, LEVD - 1) * ROWS_IN + jnp.minimum(slot, SLOTS - 1) * LON
@@ -173,6 +234,7 @@
         )
 
     masks64 = head_masks(LEV)
+    ones64 = jnp.concatenate([m.astype(BF16) for m in masks64], 0)
 
     def column_chunk(i, _):
         pltpu.make_async_copy(
@@ -183,30 +245,27 @@
             r32[pl.ds(pl.multiple_of(d * ROWS_IN, ROWS_IN), ROWS_IN), :] = recv[i, d].astype(F32)
             return 0
 
-        lax.fori_loop(0, LEVD, widen_in, 0)
+        lax.fori_loop(0, LEVD, widen_in, 0, unroll=4)
 
         def pick(level, _):
             xl[pl.ds(pl.multiple_of(level * 16, 16), 16), :] = r32[pl.ds(rowoff[level], 16), :]
             return 0
 
-        lax.fori_loop(0, LEV, pick, 0, unroll=8)
-
+        lax.fori_loop(0, LEV, pick, 0, unroll=16)
+
+        cols = jnp.concatenate([xl[pl.ds(lon, LEV, stride=16), :] for lon in range(LON)], 0)
+        packed = dot(norm(cols, gcol_ref[...]), wcq_ref[...]).astype(BF16)
+        parts = []
+        for n in range(LON):
+            one = packed[n * LEV:(n + 1) * LEV]
+            parts.append(attend_short(one[:, :C], one[:, C:2 * C], one[:, 2 * C:], masks64, ones64))
+        done = cols + dot(jnp.concatenate(parts, 0).astype(BF16), wco_ref[...])
+        normed = norm(done, gwin_ref[...])
         for half in range(2):
-            for first in range(0, HALF, COLG):
-                lons = [half * HALF + first + n for n in range(COLG)]
-                cols = jnp.concatenate([xl[pl.ds(lon, LEV, stride=16), :] for lon in lons], 0)
-                packed = dot(norm(cols, gcol_ref[...]), wcq_ref[...]).astype(BF16)
-                parts = []
-                for n in range(COLG):
-                    one = packed[n * LEV:(n + 1) * LEV]
-                    parts.append(attend(one[:, :C], one[:, C:2 * C], one[:, 2 * C:], masks64))
-                attended = jnp.concatenate(parts, 0).astype(BF16)
-                done = cols + dot(attended, wco_ref[...])
-                normed = norm(done, gwin_ref[...])
-                for n in range(COLG):
-                    at = half * HROWS + i * HALF + first + n
-                    after[pl.ds(at, LEV, stride=COLS), :] = done[n * LEV:(n + 1) * LEV]
-                    hsend[i, half, pl.ds((first + n) * LEV, LEV), :] = normed[n * LEV:(n + 1) * LEV]
+            for n in range(HALF):
+                part = slice((half * HALF + n) * LEV, (half * HALF + n + 1) * LEV)
+                after[pl.ds(half * HROWS + i * HALF + n, LEV, stride=COLS), :] = done[part]
+                hsend[i, half, pl.ds(n * LEV, LEV), :] = normed[part]
             halo_copy(i, half, west if half == 0 else east).start()
         return 0
 
@@ -228,6 +287,8 @@
         merge_chunk(i - 1, 0)
         return 0
 
+    for weight in weights:
+        weight.wait()
     column_chunk(0, 0)
     lax.fori_loop(1, LAT, both_chunks, 0)
     merge_chunk(LAT - 1, 0)
@@ -328,7 +389,8 @@
                 r32[pl.ds(i, LEVD, stride=LAT), :] = big[
                     pl.ds(slot * COLS + i * HALF + lon, LEVD, stride=ROWS_OUT), :
                 ]
-            out_ref[slot * LON + half * HALF + lon] = r32[pl.ds(0, LATS), :].astype(BF16)
+            at = slot * LON + half * HALF + lon
+            out_ref[at] = r32[pl.ds(0, LATS), :].astype(BF16)
             return 0
 
         lax.fori_loop(0, SLOTS * HALF, unpack, 0)
@@ -353,17 +415,23 @@
     gain_mlp, w_up, w_down,
 ):
     x = levels_in.transpose(0, 2, 1, 3).reshape(ROWS_IN, LATS, C)
+    weights = [
+        gain_col.reshape(1, C), w_col_qkv, w_col_out, gain_win.reshape(1, C), w_win_qkv, w_win_out,
+        gain_mlp.reshape(1, C), w_up, w_down,
+    ]
     smem = pl.BlockSpec(memory_space=pltpu.SMEM)
     vmem = pl.BlockSpec(memory_space=pltpu.VMEM)
     dma = pltpu.SemaphoreType.DMA
     out = pl.pallas_call(
         kernel,
-        out_shape=jax.ShapeDtypeStruct((ROWS_IN, LATS, C), BF16),
-        in_specs=[smem, smem] + [vmem] * 10,
+        out_shape=pltpu.VMEM((ROWS_IN, LATS, C), BF16),
+        in_specs=[smem, smem] + [pl.BlockSpec(memory_space=pl.ANY)] * 10,
         out_specs=vmem,
         scratch_shapes=[
+            *[pltpu.VMEM(w.shape, w.dtype) for w in weights],
             pltpu.SMEM((LEV,), jnp.int32),
             pltpu.SMEM((LEVD,), jnp.int32),
+            pltpu.VMEM((ROWS_IN, LATS, C), BF16),
             pltpu.VMEM((ROWS_IN * LATS, C), F32),
             pltpu.VMEM((LAT, LEVD, ROWS_IN, C), BF16),
             pltpu.VMEM((LAT, LEVD, ROWS_IN, C), BF16),
@@ -380,6 +448,7 @@
             pltpu.VMEM((2, HROWS + PAIR, C), F32),
             pltpu.VMEM((2, LEVD, ROWS_OUT, C), BF16),
             pltpu.VMEM((2, LEVD, ROWS_OUT, C), BF16),
+            dma((SLOTS,)), dma((9,)),
             dma((LAT,)), dma((LAT,)),
             dma((LAT, 2)), dma((LAT, 2)),
             dma((2, GROUPS)), dma((2, GROUPS)),
@@ -388,10 +457,7 @@
         compiler_params=pltpu.CompilerParams(
             collective_id=0, has_side_effects=True, vmem_limit_bytes=56 * 1024 * 1024
         ),
-    )(
-        slab_levels, shifts, x, gain_col.reshape(1, C), w_col_qkv, w_col_out, gain_win.reshape(1, C),
-        w_win_qkv, w_win_out, gain_mlp.reshape(1, C), w_up, w_down,
-    )
+    )(slab_levels, shifts, x, *weights)
     return out.reshape(SLOTS, LON, LATS, C).transpose(0, 2, 1, 3)
 
 

time: 100 us -> 94.6 us (0.946)
  Pallas kernels: 96.6 us -> 93.1 us
  local copies, waits for them, and re-layouts: 3.22 us -> 1.41 us
    pallas_call x1, Pallas kernels: 96.6 us -> 93.1 us  [per_device(): pl.pallas_call(kernel, out_shape=pltpu.VMEM((ROWS_IN, LATS, C), BF16), in...]
    unnamed x1, local copies, waits for them, and re-layouts: 3.22 us -> 1.41 us
where the time goes in v2:
time: 94.6 us; the launch traced here: 94.5 us
  Pallas kernels  93.1 us (98%)
  local copies, waits for them, and re-layouts  1.41 us (1%)
    pallas_call x1, Pallas kernels, per_device(): pl.pallas_call(kernel, out_shape=pltpu.VMEM((ROWS_IN, LATS, C), BF16), in...  93.1 us

profile of v2, /device:TPU:1, one launch (start us, length us, event | category | flops | bytes accessed | tf_op | source)
XLA Modules:
  0.0 94.5 jit_solution(17262794532457843168)
XLA Ops:
  0.0 93.1 %shard_map.118 = bf16[48,192,128]{2,1,0:T(8,128)(2,1)S(1)} custom-call(s32[32]{0:T(128)} %counts_ref.1, s32[32]{0:T(128)} %shifts_ref.1, bf16[48,192,128]{2,1,0:T(8,128)(2,1)} %bitcast.10, f32[1,128]{1,0:T(1,128)} %bitcast.11, bf16[128,384]{1,0:T(8,128)(2,1)} %wcq_hbm.1, bf16[128,128]{1,0:T(8,128)(2,1)} %wco_hbm.1, f32[1,128]{1,0:T(1,128)} %bitcast.12, ...), custom_call_target="tpu_custom_call" | custom-call | tf_op jit(solution)/shard_map/pallas_call | solution.py:425
  93.1 1.4 %copy.14 = bf16[4,192,12,128]{3,1,2,0:T(8,128)(2,1)} copy(bf16[4,192,12,128]{3,1,2,0:T(8,128)(2,1)S(1)} %bitcast.9) | data formatting | bytes 4718592

commit v3 on v2

--- a/solution.py
+++ b/solution.py
@@ -118,10 +118,15 @@
     return half * jnp.tanh(inner) + half
 
 
-def plane_target(me, step):
-    core, x, y = lax.rem(me, 2), lax.rem(me // 2, 4), me // 8
-    dc, dx, dy = lax.rem(step, 2), lax.rem(step // 2, 4), step // 8
-    return (lax.rem(y + dy, 4) * 4 + lax.rem(x + dx, 4)) * 2 + lax.rem(core + dc, 2)
+CHIPS = (
+    (2, 2), (2, 1), (1, 2), (2, 3), (3, 2), (1, 1), (3, 3), (1, 3), (3, 1), (2, 0), (0, 2),
+    (0, 1), (0, 3), (1, 0), (3, 0), (0, 0),
+)
+
+
+def chip_at(me, dy, dx):
+    x, y = lax.rem(me // 2, 4), me // 8
+    return (lax.rem(y + dy, 4) * 4 + lax.rem(x + dx, 4)) * 2
 
 
 def kernel(
@@ -155,7 +160,7 @@
     ]
 
     def greet(step, _):
-        pl.semaphore_signal(barrier, inc=1, device_id={"lev": plane_target(me, step)}, device_id_type=MESH)
+        pl.semaphore_signal(barrier, inc=1, device_id={"lev": lax.rem(me + step, LEVD)}, device_id_type=MESH)
         return 0
 
     lax.fori_loop(1, LEVD, greet, 0)
@@ -178,18 +183,32 @@
             device_id={"lev": dest}, device_id_type=MESH,
         )
 
-    def send_chunk(i, _):
-        def one(step, _):
-            dest = plane_target(me, LEVD - step)
-            sendbuf[i, dest] = big[pl.ds(dest * LAT + i, ROWS_IN, stride=LATS), :].astype(BF16)
-            in_copy(i, dest).start()
-            return 0
-
-        lax.fori_loop(1, LEVD, one, 0)
+    core = lax.rem(me, 2)
+    mate = me + 1 - 2 * core
+
+    def send_to(i, dest):
+        sendbuf[i, dest] = big[pl.ds(dest * LAT + i, ROWS_IN, stride=LATS), :].astype(BF16)
+        in_copy(i, dest).start()
+
+    def send_chunk(i, _, turn):
+        for dy, dx in CHIPS[:-1]:
+            send_to(i, chip_at(me, dy, dx) + turn)
+
+        @pl.when(core != turn)
+        def _():
+            send_to(i, mate)
+
+        return 0
+
+    def keep_chunk(i, _):
         recv[i, me] = big[pl.ds(me * LAT + i, ROWS_IN, stride=LATS), :].astype(BF16)
         return 0
 
-    lax.fori_loop(0, LAT, send_chunk, 0)
+    lax.fori_loop(0, LAT, functools.partial(send_chunk, turn=0), 0)
+
+    lax.fori_loop(0, LAT, functools.partial(send_chunk, turn=1), 0)
+
+    lax.fori_loop(0, LAT, keep_chunk, 0)
 
     for weight in weights:
         weight.start()
@@ -363,14 +382,16 @@
             rows = blk[half, pl.ds(starts[dest] * COLS, ROWS_OUT), :]
             return jnp.where(row < counts_ref[dest] * COLS, rows, 0.0).astype(BF16)
 
-        def send_out(step, _):
-            dest = plane_target(me, LEVD - step)
+        def fill(dest, _):
             msg[half, dest] = block_for(dest)
-            out_copy(half, dest).start()
-            return 0
-
-        lax.fori_loop(1, LEVD, send_out, 0)
-        got[half, me] = block_for(me)
+            return 0
+
+        lax.fori_loop(0, LEVD, fill, 0)
+        for dy, dx in CHIPS[:-1]:
+            for turn in range(2):
+                out_copy(half, chip_at(me, dy, dx) + turn).start()
+        out_copy(half, mate).start()
+        got[half, me] = msg[half, me]
 
     for half in range(2):
         pltpu.make_async_copy(

time: 94.6 us -> 87.1 us (0.921)
  Pallas kernels: 93.1 us -> 85.6 us
    pallas_call x1, Pallas kernels: 93.1 us -> 85.6 us  [per_device(): pl.pallas_call(kernel, out_shape=pltpu.VMEM((ROWS_IN, LATS, C), BF16), in...]
where the time goes in v3:
time: 87.1 us; the launch traced here: 87 us
  Pallas kernels  85.6 us (98%)
  local copies, waits for them, and re-layouts  1.41 us (2%)
    pallas_call x1, Pallas kernels, per_device(): pl.pallas_call(kernel, out_shape=pltpu.VMEM((ROWS_IN, LATS, C), BF16), in...  85.6 us

profile of v3, /device:TPU:1, one launch (start us, length us, event | category | flops | bytes accessed | tf_op | source)
XLA Modules:
  0.0 87.0 jit_solution(7821099820384728960)
XLA Ops:
  0.0 85.6 %shard_map.118 = bf16[48,192,128]{2,1,0:T(8,128)(2,1)S(1)} custom-call(s32[32]{0:T(128)} %counts_ref.1, s32[32]{0:T(128)} %shifts_ref.1, bf16[48,192,128]{2,1,0:T(8,128)(2,1)} %bitcast.10, f32[1,128]{1,0:T(1,128)} %bitcast.11, bf16[128,384]{1,0:T(8,128)(2,1)} %wcq_hbm.1, bf16[128,128]{1,0:T(8,128)(2,1)} %wco_hbm.1, f32[1,128]{1,0:T(1,128)} %bitcast.12, ...), custom_call_target="tpu_custom_call" | custom-call | tf_op jit(solution)/shard_map/pallas_call | solution.py:446
  85.6 1.4 %copy.14 = bf16[4,192,12,128]{3,1,2,0:T(8,128)(2,1)} copy(bf16[4,192,12,128]{3,1,2,0:T(8,128)(2,1)S(1)} %bitcast.9) | data formatting | bytes 4718592

commit v4 on v3

--- a/solution.py
+++ b/solution.py
@@ -301,16 +301,10 @@
                 wtok[pl.ds(at, LEV, stride=COLS), :] = jnp.where(own, mine, other)
         return 0
 
-    def both_chunks(i, _):
-        column_chunk(i, 0)
-        merge_chunk(i - 1, 0)
-        return 0
-
     for weight in weights:
         weight.wait()
-    column_chunk(0, 0)
-    lax.fori_loop(1, LAT, both_chunks, 0)
-    merge_chunk(LAT - 1, 0)
+    lax.fori_loop(0, LAT, column_chunk, 0)
+    lax.fori_loop(0, LAT, merge_chunk, 0)
 
     masks144 = head_masks(PAIR)
 

time: 87.1 us -> 83.8 us (0.962)
  Pallas kernels: 85.6 us -> 82.3 us
    pallas_call x1, Pallas kernels: 85.6 us -> 82.3 us  [per_device(): pl.pallas_call(kernel, out_shape=pltpu.VMEM((ROWS_IN, LATS, C), BF16), in...]
where the time goes in v4:
time: 83.8 us; the launch traced here: 83.7 us
  Pallas kernels  82.3 us (98%)
  local copies, waits for them, and re-layouts  1.41 us (2%)
    pallas_call x1, Pallas kernels, per_device(): pl.pallas_call(kernel, out_shape=pltpu.VMEM((ROWS_IN, LATS, C), BF16), in...  82.3 us

profile of v4, /device:TPU:1, one launch (start us, length us, event | category | flops | bytes accessed | tf_op | source)
XLA Modules:
  0.0 83.7 jit_solution(15208930547282774593)
XLA Ops:
  0.0 82.3 %shard_map.118 = bf16[48,192,128]{2,1,0:T(8,128)(2,1)S(1)} custom-call(s32[32]{0:T(128)} %counts_ref.1, s32[32]{0:T(128)} %shifts_ref.1, bf16[48,192,128]{2,1,0:T(8,128)(2,1)} %bitcast.10, f32[1,128]{1,0:T(1,128)} %bitcast.11, bf16[128,384]{1,0:T(8,128)(2,1)} %wcq_hbm.1, bf16[128,128]{1,0:T(8,128)(2,1)} %wco_hbm.1, f32[1,128]{1,0:T(1,128)} %bitcast.12, ...), custom_call_target="tpu_custom_call" | custom-call | tf_op jit(solution)/shard_map/pallas_call | solution.py:440
  82.3 1.4 %copy.14 = bf16[4,192,12,128]{3,1,2,0:T(8,128)(2,1)} copy(bf16[4,192,12,128]{3,1,2,0:T(8,128)(2,1)S(1)} %bitcast.9) | data formatting | bytes 4718592

commit v5 on v4

--- a/solution.py
+++ b/solution.py
@@ -22,17 +22,19 @@
 LEV = 64
 LATS = LAT * LEVD
 C = 128
-COLS = HALF * LAT
+SUBS = 3
+PART = HALF * LAT // SUBS
+PARTS = 2 * SUBS
 ROWS_IN = SLOTS * LON
-ROWS_OUT = SLOTS * COLS
-HROWS = LEV * COLS
-PAIR = 4 * COLS
-PAIRS = LEV // 4
+ROWS_OUT = SLOTS * PART
+PROWS = LEV * PART
+BAND = 2 * PART
+SEQ = PARTS * BAND
+BANDS = LEV // 2
 GROUPS = 4
-GROUP = PAIRS // GROUPS
+GROUP = BANDS // GROUPS
+GROWS = GROUP * BAND
 HCOL = HALF * LEV
-FEED = 4
-WIN = 4
 GELU_A = math.sqrt(2.0 / math.pi)
 GELU_B = GELU_A * 0.044715
 SCALE = math.log2(math.e) / math.sqrt(C // HEADS)
@@ -234,16 +236,16 @@
 
     lax.fori_loop(0, LEV, shift_rows, 0)
 
-    row = lax.broadcasted_iota(jnp.int32, (PAIR, C), 0)
+    row = lax.broadcasted_iota(jnp.int32, (2 * BAND, C), 0)
 
     def own_rows(p, _):
-        shift = jnp.where(row < PAIR // 2, shifts_ref[2 * p], shifts_ref[2 * p + 1])
+        shift = jnp.where(row < BAND, shifts_ref[2 * p], shifts_ref[2 * p + 1])
         for half in range(2):
             own = (lax.rem(row, HALF) + half * HALF >= shift) == (shift <= HALF)
-            mask[half, pl.ds(pl.multiple_of(p * PAIR, PAIR), PAIR), :] = own.astype(jnp.int32)
-        return 0
-
-    lax.fori_loop(0, PAIRS, own_rows, 0)
+            mask[half, pl.ds(pl.multiple_of(p * 2 * BAND, 2 * BAND), 2 * BAND), :] = own.astype(jnp.int32)
+        return 0
+
+    lax.fori_loop(0, BANDS // 2, own_rows, 0)
 
     def halo_copy(i, half, side):
         return pltpu.make_async_remote_copy(
@@ -251,6 +253,9 @@
             send_sem=h_send.at[i, half], recv_sem=h_recv.at[i, half],
             device_id={"lon": side}, device_id_type=MESH,
         )
+
+    def column_at(i, half, n):
+        return (half * SUBS + i // 2) * PROWS + lax.rem(i, 2) * HALF + n
 
     masks64 = head_masks(LEV)
     ones64 = jnp.concatenate([m.astype(BF16) for m in masks64], 0)
@@ -283,7 +288,7 @@
         for half in range(2):
             for n in range(HALF):
                 part = slice((half * HALF + n) * LEV, (half * HALF + n + 1) * LEV)
-                after[pl.ds(half * HROWS + i * HALF + n, LEV, stride=COLS), :] = done[part]
+                after[pl.ds(column_at(i, half, n), LEV, stride=PART), :] = done[part]
                 hsend[i, half, pl.ds(n * LEV, LEV), :] = normed[part]
             halo_copy(i, half, west if half == 0 else east).start()
         return 0
@@ -297,8 +302,7 @@
                 own = (lon >= shift) == (shift <= HALF)
                 mine = hsend[i, half, pl.ds(n * LEV, LEV), :].astype(F32)
                 other = hrecv[i, half, pl.ds(n * LEV, LEV), :].astype(F32)
-                at = half * HROWS + i * HALF + n
-                wtok[pl.ds(at, LEV, stride=COLS), :] = jnp.where(own, mine, other)
+                wtok[pl.ds(column_at(i, half, n), LEV, stride=PART), :] = jnp.where(own, mine, other)
         return 0
 
     for weight in weights:
@@ -306,109 +310,107 @@
     lax.fori_loop(0, LAT, column_chunk, 0)
     lax.fori_loop(0, LAT, merge_chunk, 0)
 
-    masks144 = head_masks(PAIR)
+    masks_seq = head_masks(SEQ)
 
     def back_copy(g, half, side):
-        part = pl.ds(pl.multiple_of(g * (GROUP * PAIR), GROUP * PAIR), GROUP * PAIR)
+        parts = pl.ds(half * SUBS, SUBS)
+        rows = pl.ds(pl.multiple_of(g * GROWS, GROWS), GROWS)
         return pltpu.make_async_remote_copy(
-            src_ref=attd.at[half, part], dst_ref=back.at[half, part],
+            src_ref=attd.at[parts, rows], dst_ref=back.at[parts, rows],
             send_sem=b_send.at[half, g], recv_sem=b_recv.at[half, g],
             device_id={"lon": side}, device_id_type=MESH,
         )
 
-    def window_pair(p, _):
-        rows = WIN * PAIR
-        at = pl.multiple_of(p * rows, rows)
-        quarters = []
-        for band in range(2 * WIN):
-            for half in range(2):
-                quarters.append(wtok[pl.ds(at + half * HROWS + band * (PAIR // 2), PAIR // 2), :])
-        tokens = jnp.concatenate(quarters, 0).astype(BF16)
+    def window_group(g, _):
+        at = pl.multiple_of(g * GROWS, GROWS)
+        pieces = []
+        for band in range(GROUP):
+            for part in range(PARTS):
+                pieces.append(wtok[pl.ds(part * PROWS + at + band * BAND, BAND), :])
+        tokens = jnp.concatenate(pieces, 0).astype(BF16)
         packed = dot(tokens, wwq_ref[...]).astype(BF16)
         bands = []
-        for band in range(2 * WIN):
-            one = packed[band * PAIR:(band + 1) * PAIR]
-            bands.append(attend(one[:, :C], one[:, C:2 * C], one[:, 2 * C:], masks144))
-        for half in range(2):
-            part = slice(half * (PAIR // 2), (half + 1) * (PAIR // 2))
-            attd[half, pl.ds(at, rows), :] = jnp.concatenate([b[part] for b in bands], 0).astype(BF16)
-        return 0
-
-    def window_group(g, _):
-        lax.fori_loop(g * (GROUP // WIN), (g + 1) * (GROUP // WIN), window_pair, 0)
+        for band in range(GROUP):
+            one = packed[band * SEQ:(band + 1) * SEQ]
+            bands.append(attend(one[:, :C], one[:, C:2 * C], one[:, 2 * C:], masks_seq))
+        for part in range(PARTS):
+            rows = slice(part * BAND, (part + 1) * BAND)
+            attd[part, pl.ds(at, GROWS), :] = jnp.concatenate([b[rows] for b in bands], 0).astype(BF16)
         back_copy(g, 0, east).start()
         back_copy(g, 1, west).start()
         return 0
 
     lax.fori_loop(0, GROUPS, window_group, 0)
 
-    def out_copy(half, dest):
+    def out_copy(part, dest):
         return pltpu.make_async_remote_copy(
-            src_ref=msg.at[half, dest], dst_ref=got.at[half, me],
-            send_sem=o_send.at[half], recv_sem=o_recv.at[half],
+            src_ref=msg.at[part, dest], dst_ref=got.at[part, me],
+            send_sem=o_send.at[part], recv_sem=o_recv.at[part],
             device_id={"lev": dest}, device_id_type=MESH,
         )
 
-    for half in range(2):
-
-        def feed_pair(p, _):
-            rows = FEED * PAIR
-            at = pl.multiple_of(p * rows, rows)
-            attended = jnp.where(
-                mask[half, pl.ds(at, rows), :] > 0,
-                attd[half, pl.ds(at, rows), :].astype(F32),
-                back[half, pl.ds(at, rows), :].astype(F32),
-            ).astype(BF16)
-            stay = after[pl.ds(at + half * HROWS, rows), :] + dot(attended, wwo_ref[...])
-            hidden = gelu(dot(norm(stay, gmlp_ref[...]), wup_ref[...]))
-            blk[half, pl.ds(at, rows), :] = stay + dot(hidden.astype(BF16), wdn_ref[...])
-            return 0
-
-        def feed_group(g, _):
-            back_copy(g, half, east if half == 0 else west).wait_recv()
-            lax.fori_loop(g * (GROUP // FEED), (g + 1) * (GROUP // FEED), feed_pair, 0)
-            return 0
-
-        blk[half, pl.ds(HROWS, PAIR), :] = jnp.zeros((PAIR, C), F32)
-        lax.fori_loop(0, GROUPS, feed_group, 0)
-
-        def block_for(dest):
-            rows = blk[half, pl.ds(starts[dest] * COLS, ROWS_OUT), :]
-            return jnp.where(row < counts_ref[dest] * COLS, rows, 0.0).astype(BF16)
+    def feed_part(part, _):
+        half = part // SUBS
+        attended = jnp.where(
+            mask[half] > 0, attd[part].astype(F32), back[part].astype(F32)
+        ).astype(BF16)
+        stay = after[pl.ds(pl.multiple_of(part * PROWS, PROWS), PROWS), :] + dot(attended, wwo_ref[...])
+        hidden = gelu(dot(norm(stay, gmlp_ref[...]), wup_ref[...]))
+        blk[pl.ds(0, PROWS), :] = stay + dot(hidden.astype(BF16), wdn_ref[...])
 
         def fill(dest, _):
-            msg[half, dest] = block_for(dest)
+            rows = blk[pl.ds(starts[dest] * PART, ROWS_OUT), :]
+            msg[part, dest] = jnp.where(row < counts_ref[dest] * PART, rows, 0.0).astype(BF16)
             return 0
 
         lax.fori_loop(0, LEVD, fill, 0)
         for dy, dx in CHIPS[:-1]:
             for turn in range(2):
-                out_copy(half, chip_at(me, dy, dx) + turn).start()
-        out_copy(half, mate).start()
-        got[half, me] = msg[half, me]
-
+                out_copy(part, chip_at(me, dy, dx) + turn).start()
+        out_copy(part, mate).start()
+        got[part, me] = msg[part, me]
+        return 0
+
+    blk[pl.ds(PROWS, ROWS_OUT), :] = jnp.zeros((ROWS_OUT, C), F32)
     for half in range(2):
+        for g in range(GROUPS):
+            back_copy(g, half, east if half == 0 else west).wait_recv()
+        lax.fori_loop(half * SUBS, (half + 1) * SUBS, feed_part, 0)
+
+    stage = LEVD * ROWS_OUT
+
+    def take_part(part, _):
         pltpu.make_async_copy(
-            got.at[half, pl.ds(0, LEVD - 1)], got.at[half, pl.ds(0, LEVD - 1)], o_recv.at[half]
+            got.at[part, pl.ds(0, LEVD - 1)], got.at[part, pl.ds(0, LEVD - 1)], o_recv.at[part]
         ).wait()
 
         def widen_out(e, _):
-            big[pl.ds(pl.multiple_of(e * ROWS_OUT, ROWS_OUT), ROWS_OUT), :] = got[half, e].astype(F32)
-            return 0
-
-        lax.fori_loop(0, LEVD, widen_out, 0)
-
-        def unpack(n, _):
+            big[pl.ds(pl.multiple_of(e * ROWS_OUT, ROWS_OUT), ROWS_OUT), :] = got[part, e].astype(F32)
+            return 0
+
+        lax.fori_loop(0, LEVD, widen_out, 0, unroll=4)
+
+        def sort(n, _):
             slot, lon = n // HALF, lax.rem(n, HALF)
-            for i in range(LAT):
-                r32[pl.ds(i, LEVD, stride=LAT), :] = big[
-                    pl.ds(slot * COLS + i * HALF + lon, LEVD, stride=ROWS_OUT), :
+            for i in range(2):
+                big[pl.ds(stage + n * LATS + lax.rem(part, SUBS) * 2 + i, LEVD, stride=LAT), :] = big[
+                    pl.ds(slot * PART + i * HALF + lon, LEVD, stride=ROWS_OUT), :
                 ]
-            at = slot * LON + half * HALF + lon
-            out_ref[at] = r32[pl.ds(0, LATS), :].astype(BF16)
-            return 0
-
-        lax.fori_loop(0, SLOTS * HALF, unpack, 0)
+            return 0
+
+        lax.fori_loop(0, SLOTS * HALF, sort, 0, unroll=4)
+        return 0
+
+    for half in range(2):
+        lax.fori_loop(half * SUBS, (half + 1) * SUBS, take_part, 0)
+
+        def give(n, _):
+            slot, lon = n // HALF, lax.rem(n, HALF)
+            rows = big[pl.ds(pl.multiple_of(stage + n * LATS, LATS), LATS), :]
+            out_ref[slot * LON + half * HALF + lon] = rows.astype(BF16)
+            return 0
+
+        lax.fori_loop(0, SLOTS * HALF, give, 0, unroll=4)
 
     for i in range(LAT):
         pltpu.make_async_copy(
@@ -419,9 +421,9 @@
     for g in range(GROUPS):
         back_copy(g, 0, east).wait_send()
         back_copy(g, 1, west).wait_send()
-    for half in range(2):
+    for part in range(PARTS):
         pltpu.make_async_copy(
-            msg.at[half, pl.ds(0, LEVD - 1)], msg.at[half, pl.ds(0, LEVD - 1)], o_send.at[half]
+            msg.at[part, pl.ds(0, LEVD - 1)], msg.at[part, pl.ds(0, LEVD - 1)], o_send.at[part]
         ).wait()
 
 
@@ -453,21 +455,21 @@
             pltpu.VMEM((LEVD * ROWS_IN + 8, C), F32),
             pltpu.VMEM((LEV * 16, C), F32),
             pltpu.VMEM((LEV, C), jnp.int32),
-            pltpu.VMEM((2 * HROWS, C), F32),
+            pltpu.VMEM((PARTS * PROWS, C), F32),
             pltpu.VMEM((LAT, 2, HCOL, C), BF16),
             pltpu.VMEM((LAT, 2, HCOL, C), BF16),
-            pltpu.VMEM((2 * HROWS, C), F32),
-            pltpu.VMEM((2, HROWS, C), BF16),
-            pltpu.VMEM((2, HROWS, C), BF16),
-            pltpu.VMEM((2, HROWS, C), jnp.int32),
-            pltpu.VMEM((2, HROWS + PAIR, C), F32),
-            pltpu.VMEM((2, LEVD, ROWS_OUT, C), BF16),
-            pltpu.VMEM((2, LEVD, ROWS_OUT, C), BF16),
+            pltpu.VMEM((PARTS * PROWS, C), F32),
+            pltpu.VMEM((PARTS, PROWS, C), BF16),
+            pltpu.VMEM((PARTS, PROWS, C), BF16),
+            pltpu.VMEM((2, PROWS, C), jnp.int32),
+            pltpu.VMEM((PROWS + ROWS_OUT, C), F32),
+            pltpu.VMEM((PARTS, LEVD, ROWS_OUT, C), BF16),
+            pltpu.VMEM((PARTS, LEVD, ROWS_OUT, C), BF16),
             dma((SLOTS,)), dma((9,)),
             dma((LAT,)), dma((LAT,)),
             dma((LAT, 2)), dma((LAT, 2)),
             dma((2, GROUPS)), dma((2, GROUPS)),
-            dma((2,)), dma((2,)),
+            dma((PARTS,)), dma((PARTS,)),
         ],
         compiler_params=pltpu.CompilerParams(
             collective_id=0, has_side_effects=True, vmem_limit_bytes=56 * 1024 * 1024

time: 83.8 us -> 83.1 us (level)
  no operation moved by 1% of the time
where the time goes in v5:
time: 83.1 us; the launch traced here: 83 us
  Pallas kernels  81.6 us (98%)
  local copies, waits for them, and re-layouts  1.41 us (2%)
    pallas_call x1, Pallas kernels, per_device(): pl.pallas_call(kernel, out_shape=pltpu.VMEM((ROWS_IN, LATS, C), BF16), in...  81.6 us

profile of v5, /device:TPU:1, one launch (start us, length us, event | category | flops | bytes accessed | tf_op | source)
XLA Modules:
  0.0 83.0 jit_solution(10096994804684016139)
XLA Ops:
  0.0 81.6 %shard_map.118 = bf16[48,192,128]{2,1,0:T(8,128)(2,1)S(1)} custom-call(s32[32]{0:T(128)} %counts_ref.1, s32[32]{0:T(128)} %shifts_ref.1, bf16[48,192,128]{2,1,0:T(8,128)(2,1)} %bitcast.10, f32[1,128]{1,0:T(1,128)} %bitcast.11, bf16[128,384]{1,0:T(8,128)(2,1)} %wcq_hbm.1, bf16[128,128]{1,0:T(8,128)(2,1)} %wco_hbm.1, f32[1,128]{1,0:T(1,128)} %bitcast.12, ...), custom_call_target="tpu_custom_call" | custom-call | tf_op jit(solution)/shard_map/pallas_call | solution.py:442
  81.6 1.4 %copy.14 = bf16[4,192,12,128]{3,1,2,0:T(8,128)(2,1)} copy(bf16[4,192,12,128]{3,1,2,0:T(8,128)(2,1)S(1)} %bitcast.9) | data formatting | bytes 4718592

commit v6 on v5

--- a/solution.py
+++ b/solution.py
@@ -31,7 +31,7 @@
 BAND = 2 * PART
 SEQ = PARTS * BAND
 BANDS = LEV // 2
-GROUPS = 4
+GROUPS = 8
 GROUP = BANDS // GROUPS
 GROWS = GROUP * BAND
 HCOL = HALF * LEV
@@ -57,20 +57,6 @@
 def head_masks(rows):
     lane = lax.broadcasted_iota(jnp.int32, (rows, C), 1)
     return [(lane // (C // HEADS)) == h for h in range(HEADS)]
-
-
-def attend(q, k, v, masks):
-    n = q.shape[0]
-    value = jnp.concatenate([v, jnp.ones((n, C), BF16)], 1)
-    over, under = None, None
-    for h in range(HEADS):
-        scores = dot_nt(jnp.where(masks[h], q, jnp.zeros_like(q)), k)
-        top = jnp.max(scores, -1, keepdims=True)
-        probs = jnp.exp2((scores - top) * SCALE).astype(BF16)
-        both = dot(probs, value)
-        over = both[:, :C] if h == 0 else jnp.where(masks[h], both[:, :C], over)
-        under = both[:, C:] if h == 0 else jnp.where(masks[h], both[:, C:], under)
-    return over / under
 
 
 def attend_short(q, k, v, masks, ones):
@@ -93,23 +79,27 @@
 
 
 def attend_long(q, k, v, masks, tail_masks, ones, tail_ones):
-    n = q.shape[0]
-    extra = n - C
+    extra = SEQ - C
+    tail_of = [m[:extra] for m in masks]
     km, kt, vm, vt = k[:C], k[C:], v[:C], v[C:]
     zero, none = jnp.zeros_like(km), jnp.zeros_like(kt)
-    tail = dot_nt(q, jnp.concatenate([jnp.where(m[:extra], kt, none) for m in masks], 0))
-    tails = jnp.zeros((n, HEADS * extra), F32)
-    total = None
-    for h in range(HEADS):
-        scores = dot_nt(q, jnp.where(masks[h], km, zero))
-        mine = jnp.where(tail_masks[h], tail, -jnp.inf)
-        top = jnp.max(jnp.maximum(scores, jnp.concatenate([mine, jnp.full((n, C - HEADS * extra), -jnp.inf, F32)], 1)), -1, keepdims=True)
-        probs = jnp.exp2((scores - top) * SCALE).astype(BF16)
-        tails = jnp.where(tail_masks[h], top, tails)
-        part = dot(probs, jnp.concatenate([jnp.where(masks[h], vm, zero), ones[h]], 1))
+    pad = jnp.zeros((C - HEADS * extra, C), BF16)
+    tail = dot_nt(q, jnp.concatenate([jnp.where(m, kt, none) for m in tail_of] + [pad], 0))
+    tops, total = jnp.zeros((SEQ, C), F32), None
+    for first in range(0, HEADS, 2):
+        heads = (first, first + 1)
+        scores = dot_nt(q, jnp.concatenate([jnp.where(masks[h], km, zero) for h in heads], 0))
+        probs = []
+        for n, h in enumerate(heads):
+            mine = scores[:, n * C:(n + 1) * C]
+            top = jnp.max(jnp.maximum(mine, jnp.where(tail_masks[h], tail, -jnp.inf)), -1, keepdims=True)
+            probs.append(jnp.exp2((mine - top) * SCALE).astype(BF16))
+            tops = jnp.where(tail_masks[h], top, tops)
+        values = jnp.concatenate([jnp.where(masks[h], vm, zero) for h in heads], 0)
+        part = dot(jnp.concatenate(probs, 1), jnp.concatenate([values, ones[first // 2]], 1))
         total = part if total is None else total + part
-    probs = jnp.exp2((tail - tails) * SCALE).astype(BF16)
-    values = jnp.concatenate([jnp.where(m[:extra], vt, none) for m in masks], 0)
+    probs = jnp.exp2((tail - tops) * SCALE).astype(BF16)
+    values = jnp.concatenate([jnp.where(m, vt, none) for m in tail_of] + [pad], 0)
     total = total + dot(probs, jnp.concatenate([values, tail_ones], 1))
     return total[:, :C] / total[:, C:]
 
@@ -310,7 +300,15 @@
     lax.fori_loop(0, LAT, column_chunk, 0)
     lax.fori_loop(0, LAT, merge_chunk, 0)
 
-    masks_seq = head_masks(SEQ)
+    extra = SEQ - C
+    masks128 = head_masks(C)
+    ones128 = [m.astype(BF16) for m in masks128]
+    ones_pairs = [jnp.concatenate(ones128[h:h + 2], 0) for h in (0, 2)]
+    tail_ones = jnp.concatenate(
+        [m[:extra] for m in ones128] + [jnp.zeros((C - HEADS * extra, C), BF16)], 0
+    )
+    tail_lane = lax.broadcasted_iota(jnp.int32, (SEQ, C), 1) // extra
+    tail_masks = [tail_lane == h for h in range(HEADS)]
 
     def back_copy(g, half, side):
         parts = pl.ds(half * SUBS, SUBS)
@@ -332,7 +330,9 @@
         bands = []
         for band in range(GROUP):
             one = packed[band * SEQ:(band + 1) * SEQ]
-            bands.append(attend(one[:, :C], one[:, C:2 * C], one[:, 2 * C:], masks_seq))
+            bands.append(attend_long(
+                one[:, :C], one[:, C:2 * C], one[:, 2 * C:], masks128, tail_masks, ones_pairs, tail_ones
+            ))
         for part in range(PARTS):
             rows = slice(part * BAND, (part + 1) * BAND)
             attd[part, pl.ds(at, GROWS), :] = jnp.concatenate([b[rows] for b in bands], 0).astype(BF16)

time: 83.1 us -> 82.7 us (level)
  no operation moved by 1% of the time
where the time goes in v6:
time: 82.7 us; the launch traced here: 82.6 us
  Pallas kernels  81.2 us (98%)
  local copies, waits for them, and re-layouts  1.41 us (2%)
    pallas_call x1, Pallas kernels, per_device(): pl.pallas_call(kernel, out_shape=pltpu.VMEM((ROWS_IN, LATS, C), BF16), in...  81.2 us

profile of v6, /device:TPU:1, one launch (start us, length us, event | category | flops | bytes accessed | tf_op | source)
XLA Modules:
  0.0 82.6 jit_solution(13579238327479468511)
XLA Ops:
  0.0 81.2 %shard_map.118 = bf16[48,192,128]{2,1,0:T(8,128)(2,1)S(1)} custom-call(s32[32]{0:T(128)} %counts_ref.1, s32[32]{0:T(128)} %shifts_ref.1, bf16[48,192,128]{2,1,0:T(8,128)(2,1)} %bitcast.10, f32[1,128]{1,0:T(1,128)} %bitcast.11, bf16[128,384]{1,0:T(8,128)(2,1)} %wcq_hbm.1, bf16[128,128]{1,0:T(8,128)(2,1)} %wco_hbm.1, f32[1,128]{1,0:T(1,128)} %bitcast.12, ...), custom_call_target="tpu_custom_call" | custom-call | tf_op jit(solution)/shard_map/pallas_call | solution.py:442
  81.2 1.4 %copy.14 = bf16[4,192,12,128]{3,1,2,0:T(8,128)(2,1)} copy(bf16[4,192,12,128]{3,1,2,0:T(8,128)(2,1)S(1)} %bitcast.9) | data formatting | bytes 4718592

commit v7 on v6

--- a/solution.py
+++ b/solution.py
@@ -214,29 +214,6 @@
 
     lax.fori_loop(0, LEV, place, (jnp.int32(0), jnp.int32(0)))
 
-    def begin(slab, start):
-        starts[slab] = jnp.minimum(start, LEV - 1)
-        return start + counts_ref[slab]
-
-    lax.fori_loop(0, LEVD, begin, jnp.int32(0))
-
-    def shift_rows(level, _):
-        srow[pl.ds(level, 1), :] = jnp.full((1, C), shifts_ref[level // 2], jnp.int32)
-        return 0
-
-    lax.fori_loop(0, LEV, shift_rows, 0)
-
-    row = lax.broadcasted_iota(jnp.int32, (2 * BAND, C), 0)
-
-    def own_rows(p, _):
-        shift = jnp.where(row < BAND, shifts_ref[2 * p], shifts_ref[2 * p + 1])
-        for half in range(2):
-            own = (lax.rem(row, HALF) + half * HALF >= shift) == (shift <= HALF)
-            mask[half, pl.ds(pl.multiple_of(p * 2 * BAND, 2 * BAND), 2 * BAND), :] = own.astype(jnp.int32)
-        return 0
-
-    lax.fori_loop(0, BANDS // 2, own_rows, 0)
-
     def halo_copy(i, half, side):
         return pltpu.make_async_remote_copy(
             src_ref=hsend.at[i, half], dst_ref=hrecv.at[i, half],
@@ -298,6 +275,29 @@
     for weight in weights:
         weight.wait()
     lax.fori_loop(0, LAT, column_chunk, 0)
+    def begin(slab, start):
+        starts[slab] = jnp.minimum(start, LEV - 1)
+        return start + counts_ref[slab]
+
+    lax.fori_loop(0, LEVD, begin, jnp.int32(0))
+
+    def shift_rows(level, _):
+        srow[pl.ds(level, 1), :] = jnp.full((1, C), shifts_ref[level // 2], jnp.int32)
+        return 0
+
+    lax.fori_loop(0, LEV, shift_rows, 0)
+
+    row = lax.broadcasted_iota(jnp.int32, (2 * BAND, C), 0)
+
+    def own_rows(p, _):
+        shift = jnp.where(row < BAND, shifts_ref[2 * p], shifts_ref[2 * p + 1])
+        for half in range(2):
+            own = (lax.rem(row, HALF) + half * HALF >= shift) == (shift <= HALF)
+            mask[half, pl.ds(pl.multiple_of(p * 2 * BAND, 2 * BAND), 2 * BAND), :] = own.astype(jnp.int32)
+        return 0
+
+    lax.fori_loop(0, BANDS // 2, own_rows, 0)
+
     lax.fori_loop(0, LAT, merge_chunk, 0)
 
     extra = SEQ - C

time: 82.7 us -> 82.4 us (level)
  no operation moved by 1% of the time
where the time goes in v7:
time: 82.4 us; the launch traced here: 82.3 us
  Pallas kernels  80.9 us (98%)
  local copies, waits for them, and re-layouts  1.41 us (2%)
    pallas_call x1, Pallas kernels, per_device(): pl.pallas_call(kernel, out_shape=pltpu.VMEM((ROWS_IN, LATS, C), BF16), in...  80.9 us

profile of v7, /device:TPU:1, one launch (start us, length us, event | category | flops | bytes accessed | tf_op | source)
XLA Modules:
  0.0 82.3 jit_solution(10867537050867292870)
XLA Ops:
  0.0 80.9 %shard_map.118 = bf16[48,192,128]{2,1,0:T(8,128)(2,1)S(1)} custom-call(s32[32]{0:T(128)} %counts_ref.1, s32[32]{0:T(128)} %shifts_ref.1, bf16[48,192,128]{2,1,0:T(8,128)(2,1)} %bitcast.10, f32[1,128]{1,0:T(1,128)} %bitcast.11, bf16[128,384]{1,0:T(8,128)(2,1)} %wcq_hbm.1, bf16[128,128]{1,0:T(8,128)(2,1)} %wco_hbm.1, f32[1,128]{1,0:T(1,128)} %bitcast.12, ...), custom_call_target="tpu_custom_call" | custom-call | tf_op jit(solution)/shard_map/pallas_call | solution.py:442
  80.9 1.4 %copy.14 = bf16[4,192,12,128]{3,1,2,0:T(8,128)(2,1)} copy(bf16[4,192,12,128]{3,1,2,0:T(8,128)(2,1)S(1)} %bitcast.9) | data formatting | bytes 4718592
